TPU v7x, 256 devices: a whole 4x4x8 slice. The times are simulated.
256 devices in a mesh: row: 8 (over y_lo, x), col: 32 (over z, y_hi, core).
Axes of the slice: x: 4, y: 4 (y_hi: 2, y_lo: 2; y = y_hi * 2 + y_lo), z: 8, core: 2. Of those that a mesh axis runs over, the one named last changes fastest.
Arguments:
- left_features: bfloat16 [32, 2048, 320], P('row', 'col'), may hold values from -6 to 6
- right_features: bfloat16 [32, 2048, 320], P('row', 'col'), may hold values from -6 to 6
- conv_weight: bfloat16 [3, 3, 3, 40, 32], replicated, may hold values from -0.1875 to 0.1875
- cotangent: bfloat16 [24, 32, 2048, 32], P(None, 'row', 'col'), may hold values from -6 to 6
Outputs:
- cost_output: bfloat16 [24, 32, 2048, 32], P(None, 'row', 'col')
- weight_grad: float32 [3, 3, 3, 40, 32], replicated
- left_grad: bfloat16 [32, 2048, 320], P('row', 'col')
- right_grad: bfloat16 [32, 2048, 320], P('row', 'col')
All inputs are finite; a program needn't handle non-finite values.
Results may differ from a plain program's by a relative error of at most 0.0049.
Values may be sent and summed in bfloat16 or wider, within the bound.
A program may use at most 128 MiB of HBM per device.

v0:
```python
import math
import jax
import jax.numpy as jnp
from jax import lax
from jax.sharding import PartitionSpec as P

DISP = 24
STEP = 4
DIMS = ("NDHWC", "DHWIO", "NDHWC")
KERNEL_DIMS = ("CDHWN", "IDHWO", "NDHWC")


def shifted_2(block, axis, distance):
    devices = range(lax.axis_size(axis))
    route = [(i - distance, i) for i in devices if i - distance in devices]
    return lax.ppermute(block, axis, route)


def with_halo(cells, sides, width):
    for axis, dim in sides:
        count = lax.axis_size(axis)
        ends = count - 1
        head = lax.slice_in_dim(cells, 0, width, axis=dim)
        tail = lax.slice_in_dim(cells, cells.shape[dim] - width, cells.shape[dim], axis=dim)
        cells = jnp.concatenate(
            [
                lax.ppermute(tail, axis, [(i, (i + 1) % count) for i in range(ends)]),
                cells,
                lax.ppermute(head, axis, [((i + 1) % count, i) for i in range(ends)]),
            ],
            axis=dim,
        )
    return cells


def conv_valid(padded_input, kernel):
    return lax.conv_general_dilated(
        padded_input[None],
        kernel,
        (1, 1, 1),
        ((1, 1), (0, 0), (0, 0)),
        dimension_numbers=DIMS,
        preferred_element_type=jnp.float32,
    )[0]


def on_device(left_features, right_features, conv_weight, cotangent):
    tile_rows, tile_cols, channels = left_features.shape
    groups = conv_weight.shape[3]
    group_size = channels // groups
    reach_cols = STEP * (DISP - 1)
    hop_count = -(-reach_cols // tile_cols)
    band_base = hop_count * tile_cols
    band_width = band_base + tile_cols
    pieces = [right_features]
    carried = right_features
    for hop_index in range(hop_count):
        carried = shifted_2(carried, "col", 1)
        pieces.insert(0, carried)
    right_band = jnp.concatenate(pieces, axis=1)
    group_table = (
        jnp.arange(channels)[:, None] // group_size == jnp.arange(groups)[None, :]
    ).astype(jnp.float32)
    left_float = left_features.astype(jnp.float32)
    planes = []
    for disp_index in range(DISP):
        band_start = band_base - STEP * disp_index
        shifted = right_band[:, band_start : band_start + tile_cols].astype(jnp.float32)
        planes.append(
            jnp.einsum(
                "hwc,cg->hwg", left_float * shifted, group_table, precision=lax.Precision.HIGHEST
            )
        )
    volume = (jnp.stack(planes) / group_size).astype(jnp.bfloat16)
    padded_volume = with_halo(volume, (("row", 1), ("col", 2)), 1)
    output = conv_valid(padded_volume, conv_weight).astype(jnp.bfloat16)
    padded_cotangent = with_halo(cotangent, (("row", 1), ("col", 2)), 1)
    flipped = jnp.transpose(conv_weight[::-1, ::-1, ::-1], (0, 1, 2, 4, 3))
    grad_volume = conv_valid(padded_cotangent, flipped).astype(jnp.bfloat16)
    full_pad = jnp.pad(padded_volume, ((1, 1), (0, 0), (0, 0), (0, 0)))
    kernel_raw = lax.conv_general_dilated(
        full_pad[None],
        cotangent[None],
        (1, 1, 1),
        ((0, 0), (0, 0), (0, 0)),
        dimension_numbers=KERNEL_DIMS,
        preferred_element_type=jnp.float32,
    )
    local_grad = jnp.transpose(kernel_raw, (1, 2, 3, 0, 4))
    total_cells = DISP * tile_rows * lax.axis_size("row") * tile_cols * lax.axis_size("col")
    weight_grad = lax.psum(local_grad, ("row", "col")) / math.sqrt(total_cells)
    left_accum = jnp.zeros((tile_rows, tile_cols, channels), jnp.float32)
    grad_band = jnp.zeros((tile_rows, band_width, channels), jnp.float32)
    for disp_index in range(DISP):
        band_start = band_base - STEP * disp_index
        shifted = right_band[:, band_start : band_start + tile_cols].astype(jnp.float32)
        spread = jnp.einsum(
            "hwg,cg->hwc",
            grad_volume[disp_index].astype(jnp.float32),
            group_table,
            precision=lax.Precision.HIGHEST,
        )
        left_accum = left_accum + spread * shifted
        contrib = spread * left_float
        grad_band = grad_band + jnp.pad(
            contrib, ((0, 0), (band_start, band_width - band_start - tile_cols), (0, 0))
        )

    def band_piece(hop_index):
        return grad_band[
            :, band_base - hop_index * tile_cols : band_base - (hop_index - 1) * tile_cols
        ]

    right_accum = band_piece(hop_count)
    for hop_index in range(hop_count - 1, -1, -1):
        right_accum = shifted_2(right_accum, "col", -1) + band_piece(hop_index)
    left_grad = (left_accum / group_size).astype(jnp.bfloat16)
    right_grad = (right_accum / group_size).astype(jnp.bfloat16)
    return (output, weight_grad, left_grad, right_grad)


def solution(mesh):
    in_specs = (P("row", "col", None), P("row", "col", None), P(), P(None, "row", "col", None))
    out_specs = (P(None, "row", "col", None), P(), P("row", "col", None), P("row", "col", None))
    return jax.shard_map(
        on_device, mesh=mesh, in_specs=in_specs, out_specs=out_specs, check_vma=False
    )
```

profile of v0, /device:TPU:1, one launch (start us, length us, event | category | flops | bytes accessed | tf_op | source)
XLA Modules:
  0.0 492.1 jit_solution(12546032081893617520)
XLA Ops:
  7.2 2.0 copy.212
  9.3 4.1 collective-permute-start.6
  13.4 1.3 collective-permute-start.7
  14.7 5.7 %collective-permute-start = (bf16[4,64,320]{2,1,0:T(8,128)(2,1)S(1)}, bf16[4,64,320]{2,1,0:T(8,128)(2,1)}, u32[]{:S(2)}, u32[]{:S(2)}) collective-permute-start(bf16[4,64,320]{2,1,0:T(8,128)(2,1)S(1)} %copy-done.27), channel_id=1, source_target_pairs={{0,1},{1,2},{2,3},{3,4},{4,5},{5,6},{6,7},{7,8},{8,9},{9,10},{10,1... | collective-permute-start | bytes 491528 | tf_op jit(solution)/shard_map/ppermute | solution.py:16
  21.2 3.8 collective-permute-done.7
  25.8 6.6 %collective-permute-start.8 = (bf16[24,6,1,32]{3,0,2,1:T(8,128)(2,1)S(1)}, bf16[24,6,1,32]{3,0,2,1:T(8,128)(2,1)S(1)}, u32[]{:S(2)}, u32[]{:S(2)}) collective-permute-start(bf16[24,6,1,32]{3,0,2,1:T(8,128)(2,1)S(1)} %get-tuple-element.20), channel_id=1, source_target_pairs={{0,1},{1,2},{2,3},{3,4},{4,5},{5,6},{6,7},{7,8},{8,9},{9,10},{10,1... | collective-permute-start | bytes 27656 | tf_op jit(solution)/shard_map/ppermute | solution.py:27
  32.3 1.9 collective-permute-start.9
  34.3 1.1 fusion.45
  35.4 5.1 %copy.211 = bf16[1,24,4,64,32]{4,0,3,2,1:T(2,128)(2,1)} copy(bf16[1,24,4,64,32]{3,4,2,1,0:T(8,128)(2,1)S(1)} %bitcast.279) | data formatting | bytes 786432 | tf_op jit(solution)/shard_map/broadcast_in_dim | solution.py:83
  40.5 2.5 maximum_bitcast_fusion
  44.3 5.4 %select_convert_fusion = bf16[24,4,8,9,40]{4,2,3,1,0:T(8,128)(2,1)S(1)} fusion(pred[8,9]{0,1:T(8,128)(4,1)S(1)} %copy-done.29, bf16[3,3,3,40,32]{3,4,2,1,0:T(8,128)(2,1)S(1)} %copy-done, bf16[24,6,1,7,2,32]{5,3,4,1,0,2:T(8,128)(2,1)S(1)} %slice.377, bf16[24,6,1,8,9,32]{5,3,4,1,0,2:T(8,128)(2,1)S(1)} %copy.216), kind=kOutput, calls=%fused_computation.52 | convolution fusion | flops 467472384 | bytes 1414728 | tf_op jit(solution)/shard_map/conv_general_dilated | solution.py:37
  53.8 1.0 copy.239
  55.4 0.9 copy.277
  56.4 1.0 fusion.118
  58.9 0.9 copy.276
  59.9 1.0 fusion.120
  62.4 0.9 copy.275
  63.4 1.0 fusion.122
  66.9 1.0 fusion.124
  70.4 1.1 fusion.126
  74.0 1.0 fusion.128
  77.5 1.0 fusion.130
  81.0 1.0 fusion.132
  83.6 0.9 copy.269
  84.5 1.0 fusion.134
  87.1 0.9 copy.268
  88.0 1.0 fusion.136
  90.6 0.9 copy.267
  91.5 1.0 fusion.138
  95.2 1.0 fusion.100
  96.4 1.0 fusion.102
  97.5 1.0 fusion.104
  99.1 6.1 %convert_multiply_fusion.23 = (f32[4,64,320]{2,1,0:T(8,128)}, f32[4,64,320]{2,1,0:T(8,128)}, f32[4,64,320]{2,1,0:T(8,128)}, f32[4,64,320]{2,1,0:T(8,128)}, f32[4...) fusion(bf16[4,64,320]{2,1,0:T(8,128)(2,1)S(1)} %copy-done.1, ...), kind=kOutput, calls=%fused_computation.27 | convolution fusion | flops 8122880 | bytes 11982080 | tf_op jit(solution)/shard_map/hwg,cg->hwc/dot_general | solution.py:97
  105.5 5.7 %collective-permute-start.1 = (bf16[4,64,320]{2,1,0:T(8,128)(2,1)}, bf16[4,64,320]{2,1,0:T(8,128)(2,1)S(1)}, u32[]{:S(2)}, u32[]{:S(2)}) collective-permute-start(bf16[4,64,320]{2,1,0:T(8,128)(2,1)} %collective-permute-done), channel_id=1, source_target_pairs={{0,1},{1,2},{2,3},{3,4},{4,5},{5,6},{6,7},{7,8},{8,9},{9,10},{10,1... | collective-permute-start | bytes 491528 | tf_op jit(solution)/shard_map/ppermute | solution.py:16
  111.4 2.3 collective-permute-done.1
  113.7 1.0 constant_dynamic-update-slice_fusion.2
  122.5 1.4 fusion.29
  127.9 3.4 collective-permute-start.2
  131.3 1.3 collective-permute-start.3
  132.8 3.0 multiply_convert_fusion.1
  135.8 1.5 convert_multiply_fusion.5
  137.3 1.0 collective-permute-done.3
  138.6 1.8 fusion.250
  140.4 2.3 copy.202
  142.7 7.6 %collective-permute-start.4 = (bf16[24,6,1,40]{3,0,2,1:T(8,128)(2,1)S(1)}, bf16[24,6,1,40]{3,0,2,1:T(8,128)(2,1)S(1)}, u32[]{:S(2)}, u32[]{:S(2)}) collective-permute-start(bf16[24,6,1,40]{3,0,2,1:T(8,128)(2,1)S(1)} %copy.202), channel_id=1, source_target_pairs={{0,1},{1,2},{2,3},{3,4},{4,5},{5,6},{6,7},{7,8},{8,9},{9,10},{10,1... | collective-permute-start | bytes 34568 | tf_op jit(solution)/shard_map/ppermute | solution.py:27
  150.3 0.9 copy.203
  151.3 1.9 collective-permute-start.5
  153.2 4.3 pad_add_fusion
  158.3 1.9 collective-permute-start.10
  160.3 1.0 copy.204
  161.3 2.1 copy.205
  163.4 2.7 pad_maximum_fusion.1
  166.1 1.5 pad_bitcast_fusion
  167.6 12.4 %copy.210 = bf16[1,26,6,66,40]{4,0,3,2,1:T(2,128)(2,1)} copy(bf16[1,26,6,66,40]{3,4,2,1,0:T(8,128)(2,1)} %pad_bitcast_fusion) | data formatting | bytes 1647360 | tf_op jit(solution)/shard_map/broadcast_in_dim | solution.py:82
  180.0 42.7 %fusion.252 = f32[3,3,3,40,32]{3,4,2,1,0:T(8,128)} fusion(bf16[1,26,6,66,40]{4,0,3,2,1:T(2,128)(2,1)} %copy.210, bf16[1,24,4,64,32]{4,0,3,2,1:T(2,128)(2,1)} %copy.211), kind=kOutput, calls=%fused_computation.321 | convolution fusion | flops 424673280 | bytes 1355136 | tf_op jit(solution)/shard_map/transpose | solution.py:89
  222.7 3.9 fusion.257
  226.6 3.3 copy.290
  230.9 6.0 %select_convert_fusion.1 = bf16[24,4,8,9,32]{4,2,3,1,0:T(8,128)(2,1)S(1)} fusion(pred[8,9]{0,1:T(8,128)(4,1)S(1)} %copy-done.29, bf16[3,3,3,40,32]{3,4,2,1,0:T(8,128)(2,1)S(1)} %copy-done, bf16[24,6,1,7,2,40]{5,3,4,1,0,2:T(8,128)(2,1)S(1)} %slice.373, bf16[24,6,1,8,9,40]{5,3,4,1,0,2:T(8,128)(2,1)S(1)} %copy.208), kind=kOutput, calls=%fused_computation.53 | convolution fusion | flops 467970048 | bytes 1502280 | tf_op jit(solution)/shard_map/conv_general_dilated | solution.py:37
  238.1 1.8 slice_add_fusion.1
  240.0 1.9 collective-permute-start.11
  242.2 1.7 copy.265
  243.8 237.6 %all-reduce.27.cloned.1.call-done = f32[3,3,3,40,32]{3,4,2,1,0:T(8,128)} async-done(((f32[3,3,3,40,32]{3,4,2,1,0:T(8,128)}), f32[3,3,3,40,32]{3,4,2,1,0:T(8,128)}) %all-reduce.27.cloned.1.call-update) | async-done | bytes 138256 | tf_op jit(solution)/shard_map/psum | solution.py:91
  481.5 1.8 broadcast_multiply_fusion
  483.3 1.8 fusion.70
  (185 shorter events, 46.9 us)
Async XLA Ops:
  7.2 36.9 %copy-start = (bf16[3,3,3,40,32]{3,4,2,1,0:T(8,128)(2,1)S(1)}, bf16[3,3,3,40,32]{3,4,2,1,0:T(8,128)(2,1)}, u32[]{:S(2)}) copy-start(bf16[3,3,3,40,32]{3,4,2,1,0:T(8,128)(2,1)} %param.6) | copy-start | bytes 207364
  7.2 7.6 %copy-start.27 = (bf16[4,64,320]{2,1,0:T(8,128)(2,1)S(1)}, bf16[4,64,320]{2,1,0:T(8,128)(2,1)}, u32[]{:S(2)}) copy-start(bf16[4,64,320]{2,1,0:T(8,128)(2,1)} %param.5) | copy-start | bytes 491524
  7.2 474.3 %all-reduce.27.cloned.1.call-start = ((), (), s32[]{:S(2)}) async-start(), calls=%async_computation | async-start | bytes 884736 | tf_op jit(solution)/shard_map/psum | solution.py:91
  9.2 25.1 %copy-start.1 = (bf16[4,64,320]{2,1,0:T(8,128)(2,1)S(1)}, bf16[4,64,320]{2,1,0:T(8,128)(2,1)}, u32[]{:S(2)}) copy-start(bf16[4,64,320]{2,1,0:T(8,128)(2,1)} %param.4) | copy-start | bytes 491524
  9.2 26.2 %copy-start.4 = (bf16[24,4,64,32]{2,3,1,0:T(8,128)(2,1)S(1)}, bf16[24,4,64,32]{2,3,1,0:T(8,128)(2,1)}, u32[]{:S(2)}) copy-start(bf16[24,4,64,32]{2,3,1,0:T(8,128)(2,1)} %param.7) | copy-start | bytes 1179652
  9.3 11.8 %collective-permute-start.6 = (bf16[24,1,64,32]{3,0,2,1:T(8,128)(2,1)S(1)}, bf16[24,1,64,32]{3,0,2,1:T(8,128)(2,1)S(1)}, u32[]{:S(2)}, u32[]{:S(2)}) collective-permute-start(bf16[24,1,64,32]{3,0,2,1:T(8,128)(2,1)S(1)} %get-tuple-element.46), channel_id=1, source_target_pairs={{0,32},{32,64},{64,96},{96,128},{128,160},{160,192},{192,224},{1,3... | collective-permute-start | bytes 294920 | tf_op jit(solution)/shard_map/ppermute | solution.py:27
  13.4 11.6 %collective-permute-start.7 = (bf16[24,1,64,32]{3,0,2,1:T(8,128)(2,1)S(1)}, bf16[24,1,64,32]{3,0,2,1:T(8,128)(2,1)S(1)}, u32[]{:S(2)}, u32[]{:S(2)}) collective-permute-start(bf16[24,1,64,32]{3,0,2,1:T(8,128)(2,1)S(1)} %get-tuple-element.47), channel_id=1, source_target_pairs={{32,0},{64,32},{96,64},{128,96},{160,128},{192,160},{224,192},{33,... | collective-permute-start | bytes 294920 | tf_op jit(solution)/shard_map/ppermute | solution.py:29
  14.7 90.8 %collective-permute-start = (bf16[4,64,320]{2,1,0:T(8,128)(2,1)S(1)}, bf16[4,64,320]{2,1,0:T(8,128)(2,1)}, u32[]{:S(2)}, u32[]{:S(2)}) collective-permute-start(bf16[4,64,320]{2,1,0:T(8,128)(2,1)S(1)} %copy-done.27), channel_id=1, source_target_pairs={{0,1},{1,2},{2,3},{3,4},{4,5},{5,6},{6,7},{7,8},{8,9},{9,10},{10,1... | collective-permute-start | bytes 491528 | tf_op jit(solution)/shard_map/ppermute | solution.py:16
  25.0 0.7 copy-start.23
  25.8 14.8 %collective-permute-start.8 = (bf16[24,6,1,32]{3,0,2,1:T(8,128)(2,1)S(1)}, bf16[24,6,1,32]{3,0,2,1:T(8,128)(2,1)S(1)}, u32[]{:S(2)}, u32[]{:S(2)}) collective-permute-start(bf16[24,6,1,32]{3,0,2,1:T(8,128)(2,1)S(1)} %get-tuple-element.20), channel_id=1, source_target_pairs={{0,1},{1,2},{2,3},{3,4},{4,5},{5,6},{6,7},{7,8},{8,9},{9,10},{10,1... | collective-permute-start | bytes 27656 | tf_op jit(solution)/shard_map/ppermute | solution.py:27
  32.3 8.2 %collective-permute-start.9 = (bf16[24,6,1,32]{3,0,2,1:T(8,128)(2,1)S(1)}, bf16[24,6,1,32]{3,0,2,1:T(8,128)(2,1)S(1)}, u32[]{:S(2)}, u32[]{:S(2)}) collective-permute-start(bf16[24,6,1,32]{3,0,2,1:T(8,128)(2,1)S(1)} %get-tuple-element.21), channel_id=1, source_target_pairs={{1,0},{2,1},{3,2},{4,3},{5,4},{6,5},{7,6},{8,7},{9,8},{10,9},{11,1... | collective-permute-start | bytes 27656 | tf_op jit(solution)/shard_map/ppermute | solution.py:29
  43.6 0.7 copy-start.29
  52.9 46.2 %copy-start.6 = (f32[4,64,320]{2,1,0:T(8,128)}, f32[4,64,320]{2,1,0:T(8,128)S(1)}, u32[]{:S(2)}) copy-start(f32[4,64,320]{2,1,0:T(8,128)S(1)} %fusion.112) | copy-start | bytes 983044
  53.3 45.8 %copy-start.8 = (f32[4,64,320]{2,1,0:T(8,128)}, f32[4,64,320]{2,1,0:T(8,128)S(1)}, u32[]{:S(2)}) copy-start(f32[4,64,320]{2,1,0:T(8,128)S(1)} %fusion.114) | copy-start | bytes 983044
  53.8 45.3 %copy-start.10 = (f32[4,64,320]{2,1,0:T(8,128)}, f32[4,64,320]{2,1,0:T(8,128)S(1)}, u32[]{:S(2)}) copy-start(f32[4,64,320]{2,1,0:T(8,128)S(1)} %fusion.116) | copy-start | bytes 983044
  105.2 9.5 %copy-start.5 = (f32[24,4,64,40]{2,3,1,0:T(8,128)S(1)}, f32[24,4,64,40]{2,3,1,0:T(8,128)}, u32[]{:S(2)}) copy-start(f32[24,4,64,40]{2,3,1,0:T(8,128)} %fusion.45) | copy-start | bytes 2949124
  105.5 8.2 %collective-permute-start.1 = (bf16[4,64,320]{2,1,0:T(8,128)(2,1)}, bf16[4,64,320]{2,1,0:T(8,128)(2,1)S(1)}, u32[]{:S(2)}, u32[]{:S(2)}) collective-permute-start(bf16[4,64,320]{2,1,0:T(8,128)(2,1)} %collective-permute-done), channel_id=1, source_target_pairs={{0,1},{1,2},{2,3},{3,4},{4,5},{5,6},{6,7},{7,8},{8,9},{9,10},{10,1... | collective-permute-start | bytes 491528 | tf_op jit(solution)/shard_map/ppermute | solution.py:16
  124.4 8.2 %copy-start.28 = (bf16[4,64,320]{2,1,0:T(8,128)(2,1)S(1)}, bf16[4,64,320]{2,1,0:T(8,128)(2,1)}, u32[]{:S(2)}) copy-start(bf16[4,64,320]{2,1,0:T(8,128)(2,1)} %param.5) | copy-start | bytes 491524
  124.9 7.7 %copy-start.26 = (f32[4,64,320]{2,1,0:T(8,128)S(1)}, f32[4,64,320]{2,1,0:T(8,128)}, u32[]{:S(2)}) copy-start(f32[4,64,320]{2,1,0:T(8,128)} %fusion.104) | copy-start | bytes 983044
  125.5 7.1 %copy-start.25 = (f32[4,64,320]{2,1,0:T(8,128)S(1)}, f32[4,64,320]{2,1,0:T(8,128)}, u32[]{:S(2)}) copy-start(f32[4,64,320]{2,1,0:T(8,128)} %fusion.102) | copy-start | bytes 983044
  126.0 6.6 %copy-start.22 = (f32[4,64,320]{2,1,0:T(8,128)S(1)}, f32[4,64,320]{2,1,0:T(8,128)}, u32[]{:S(2)}) copy-start(f32[4,64,320]{2,1,0:T(8,128)} %fusion.138) | copy-start | bytes 983044
  126.0 6.6 %copy-start.24 = (f32[4,64,320]{2,1,0:T(8,128)S(1)}, f32[4,64,320]{2,1,0:T(8,128)}, u32[]{:S(2)}) copy-start(f32[4,64,320]{2,1,0:T(8,128)} %fusion.100) | copy-start | bytes 983044
  126.5 6.1 %copy-start.21 = (f32[4,64,320]{2,1,0:T(8,128)S(1)}, f32[4,64,320]{2,1,0:T(8,128)}, u32[]{:S(2)}) copy-start(f32[4,64,320]{2,1,0:T(8,128)} %fusion.136) | copy-start | bytes 983044
  127.1 5.6 %copy-start.19 = (f32[4,64,320]{2,1,0:T(8,128)S(1)}, f32[4,64,320]{2,1,0:T(8,128)}, u32[]{:S(2)}) copy-start(f32[4,64,320]{2,1,0:T(8,128)} %fusion.132) | copy-start | bytes 983044
  127.1 5.6 %copy-start.20 = (f32[4,64,320]{2,1,0:T(8,128)S(1)}, f32[4,64,320]{2,1,0:T(8,128)}, u32[]{:S(2)}) copy-start(f32[4,64,320]{2,1,0:T(8,128)} %fusion.134) | copy-start | bytes 983044
  127.6 5.1 %copy-start.7 = (f32[4,64,320]{2,1,0:T(8,128)S(1)}, f32[4,64,320]{2,1,0:T(8,128)}, u32[]{:S(2)}) copy-start(f32[4,64,320]{2,1,0:T(8,128)} %copy-done.6) | copy-start | bytes 983044
  127.6 5.1 %copy-start.9 = (f32[4,64,320]{2,1,0:T(8,128)S(1)}, f32[4,64,320]{2,1,0:T(8,128)}, u32[]{:S(2)}) copy-start(f32[4,64,320]{2,1,0:T(8,128)} %copy-done.8) | copy-start | bytes 983044
  127.6 5.1 %copy-start.11 = (f32[4,64,320]{2,1,0:T(8,128)S(1)}, f32[4,64,320]{2,1,0:T(8,128)}, u32[]{:S(2)}) copy-start(f32[4,64,320]{2,1,0:T(8,128)} %copy-done.10) | copy-start | bytes 983044
  127.6 5.1 %copy-start.12 = (f32[4,64,320]{2,1,0:T(8,128)S(1)}, f32[4,64,320]{2,1,0:T(8,128)}, u32[]{:S(2)}) copy-start(f32[4,64,320]{2,1,0:T(8,128)} %fusion.118) | copy-start | bytes 983044
  127.6 5.1 %copy-start.13 = (f32[4,64,320]{2,1,0:T(8,128)S(1)}, f32[4,64,320]{2,1,0:T(8,128)}, u32[]{:S(2)}) copy-start(f32[4,64,320]{2,1,0:T(8,128)} %fusion.120) | copy-start | bytes 983044
  127.7 5.1 %copy-start.14 = (f32[4,64,320]{2,1,0:T(8,128)S(1)}, f32[4,64,320]{2,1,0:T(8,128)}, u32[]{:S(2)}) copy-start(f32[4,64,320]{2,1,0:T(8,128)} %fusion.122) | copy-start | bytes 983044
  127.7 5.1 %copy-start.15 = (f32[4,64,320]{2,1,0:T(8,128)S(1)}, f32[4,64,320]{2,1,0:T(8,128)}, u32[]{:S(2)}) copy-start(f32[4,64,320]{2,1,0:T(8,128)} %fusion.124) | copy-start | bytes 983044
  127.7 5.1 %copy-start.16 = (f32[4,64,320]{2,1,0:T(8,128)S(1)}, f32[4,64,320]{2,1,0:T(8,128)}, u32[]{:S(2)}) copy-start(f32[4,64,320]{2,1,0:T(8,128)} %fusion.126) | copy-start | bytes 983044
  127.7 5.1 %copy-start.17 = (f32[4,64,320]{2,1,0:T(8,128)S(1)}, f32[4,64,320]{2,1,0:T(8,128)}, u32[]{:S(2)}) copy-start(f32[4,64,320]{2,1,0:T(8,128)} %fusion.128) | copy-start | bytes 983044
  127.7 5.1 %copy-start.18 = (f32[4,64,320]{2,1,0:T(8,128)S(1)}, f32[4,64,320]{2,1,0:T(8,128)}, u32[]{:S(2)}) copy-start(f32[4,64,320]{2,1,0:T(8,128)} %fusion.130) | copy-start | bytes 983044
  127.9 9.3 %collective-permute-start.2 = (bf16[24,1,64,40]{2,3,1,0:T(8,128)(2,1)S(1)}, bf16[24,1,64,40]{2,3,1,0:T(8,128)(2,1)S(1)}, u32[]{:S(2)}, u32[]{:S(2)}) collective-permute-start(bf16[24,1,64,40]{2,3,1,0:T(8,128)(2,1)S(1)} %get-tuple-element.50), channel_id=1, source_target_pairs={{0,32},{32,64},{64,96},{96,128},{128,160},{160,192},{192,224},{1,3... | collective-permute-start | bytes 368648 | tf_op jit(solution)/shard_map/ppermute | solution.py:27
  131.3 6.9 %collective-permute-start.3 = (bf16[24,1,64,40]{2,3,1,0:T(8,128)(2,1)S(1)}, bf16[24,1,64,40]{2,3,1,0:T(8,128)(2,1)S(1)}, u32[]{:S(2)}, u32[]{:S(2)}) collective-permute-start(bf16[24,1,64,40]{2,3,1,0:T(8,128)(2,1)S(1)} %get-tuple-element.51), channel_id=1, source_target_pairs={{32,0},{64,32},{96,64},{128,96},{160,128},{192,160},{224,192},{33,... | collective-permute-start | bytes 368648 | tf_op jit(solution)/shard_map/ppermute | solution.py:29
  142.7 17.6 %collective-permute-start.4 = (bf16[24,6,1,40]{3,0,2,1:T(8,128)(2,1)S(1)}, bf16[24,6,1,40]{3,0,2,1:T(8,128)(2,1)S(1)}, u32[]{:S(2)}, u32[]{:S(2)}) collective-permute-start(bf16[24,6,1,40]{3,0,2,1:T(8,128)(2,1)S(1)} %copy.202), channel_id=1, source_target_pairs={{0,1},{1,2},{2,3},{3,4},{4,5},{5,6},{6,7},{7,8},{8,9},{9,10},{10,1... | collective-permute-start | bytes 34568 | tf_op jit(solution)/shard_map/ppermute | solution.py:27
  151.3 10.0 %collective-permute-start.5 = (bf16[24,6,1,40]{3,0,2,1:T(8,128)(2,1)S(1)}, bf16[24,6,1,40]{3,0,2,1:T(8,128)(2,1)S(1)}, u32[]{:S(2)}, u32[]{:S(2)}) collective-permute-start(bf16[24,6,1,40]{3,0,2,1:T(8,128)(2,1)S(1)} %copy.203), channel_id=1, source_target_pairs={{1,0},{2,1},{3,2},{4,3},{5,4},{6,5},{7,6},{8,7},{9,8},{10,9},{11,1... | collective-permute-start | bytes 34568 | tf_op jit(solution)/shard_map/ppermute | solution.py:29
  157.5 2.8 copy-start.2
  158.3 79.3 %collective-permute-start.10 = (f32[4,64,320]{2,1,0:T(8,128)}, f32[4,64,320]{2,1,0:T(8,128)}, u32[]{:S(2)}, u32[]{:S(2)}) collective-permute-start(f32[4,64,320]{2,1,0:T(8,128)} %slice.426), channel_id=1, source_target_pairs={{1,0},{2,1},{3,2},{4,3},{5,4},{6,5},{7,6},{8,7},{9,8},{10,9},{11,1... | collective-permute-start | bytes 983048 | tf_op jit(solution)/shard_map/ppermute | solution.py:16
  236.9 1.3 copy-start.3
  240.0 243.3 %collective-permute-start.11 = (f32[4,64,320]{2,1,0:T(8,128)}, f32[4,64,320]{2,1,0:T(8,128)}, u32[]{:S(2)}, u32[]{:S(2)}) collective-permute-start(f32[4,64,320]{2,1,0:T(8,128)} %slice_add_fusion.1), channel_id=1, source_target_pairs={{1,0},{2,1},{3,2},{4,3},{5,4},{6,5},{7,6},{8,7},{9,8},{10,9},{11,1... | collective-permute-start | bytes 983048 | tf_op jit(solution)/shard_map/ppermute | solution.py:16
Sparse Core Ops, SparseCore 0:
  222.9 258.5 all-reduce.26
where the time goes:
time: 497 us; the launch traced here: 492 us
  waiting for transfers between devices  245 us (49%)
  matrix products  93 us (19%)
  local copies, waits for them, and re-layouts  74 us (15%)
  starting transfers between devices  43.3 us (9%)
  other arithmetic  20.8 us (4%)
  between operations  15.6 us (3%)
    psum x1, waiting for transfers between devices, on_device(): weight_grad = lax.psum(local_grad, ('row', 'col')) / math.sqrt(total_cells)  238 us
    transpose x1, matrix products, on_device(): local_grad = jnp.transpose(kernel_raw, (1, 2, 3, 0, 4))  42.7 us
    dot_general x24, matrix products, on_device(): jnp.einsum('hwg,cg->hwc', grad_volume[disp_index].astype(jnp.float32), gr...  25.2 us
    ppermute x4, starting transfers between devices, with_halo(): lax.ppermute(tail, axis, [(i, (i + 1) % count) for i in range(ends)])  21.7 us
    convert_element_type x50, local copies, waits for them, and re-layouts, on_device(): grad_volume = conv_valid(padded_cotangent, flipped).astype(jnp.bfloat16)  21.1 us
    unnamed x88, local copies, waits for them, and re-layouts  20.9 us
    ppermute x4, starting transfers between devices, shifted_2(): return lax.ppermute(block, axis, route)  15.2 us
    broadcast_in_dim x2, local copies, waits for them, and re-layouts, on_device(): full_pad[None]  13.9 us
  transfers between devices with their start and end apart: 13, of which 5 were waited for; matrix products, arithmetic and copies ran while one was open for 33% of the time, Pallas kernels for 0%

commit v1 on v0

--- a/solution.py
+++ b/solution.py
@@ -1,3 +1,4 @@
+import functools
 import math
 import jax
 import jax.numpy as jnp
@@ -8,6 +9,13 @@
 STEP = 4
 DIMS = ("NDHWC", "DHWIO", "NDHWC")
 KERNEL_DIMS = ("CDHWN", "IDHWO", "NDHWC")
+
+
+def start_fields_over_axis(buf, named_axis):
+    return jnp.sum(lax.all_gather(buf, axis_name=named_axis), axis=0)
+
+
+_recover_rows = functools.partial(start_fields_over_axis, named_axis=("row", "col"))
 
 
 def shifted_2(block, axis, distance):
@@ -88,7 +96,7 @@
     )
     local_grad = jnp.transpose(kernel_raw, (1, 2, 3, 0, 4))
     total_cells = DISP * tile_rows * lax.axis_size("row") * tile_cols * lax.axis_size("col")
-    weight_grad = lax.psum(local_grad, ("row", "col")) / math.sqrt(total_cells)
+    weight_grad = _recover_rows(local_grad) / math.sqrt(total_cells)
     left_accum = jnp.zeros((tile_rows, tile_cols, channels), jnp.float32)
     grad_band = jnp.zeros((tile_rows, band_width, channels), jnp.float32)
     for disp_index in range(DISP):

time: 497 us -> 826 us (1.66); the launches traced: 492 us -> 812 us
  waiting for transfers between devices: 245 us -> 572 us
  other arithmetic: 20.8 us -> 54 us
  local copies, waits for them, and re-layouts: 74 us -> 50 us
  matrix products: 93 us -> 76.5 us
    all_gather x0 -> x1, waiting for transfers between devices: none -> 535 us  [start_fields_over_axis(): return jnp.sum(lax.all_gather(buf, axis_name=named_axis), axis=0)]
    psum x1 -> x0, waiting for transfers between devices: 238 us -> none  [on_device(): weight_grad = lax.psum(local_grad, ('row', 'col')) / math.sqrt(total_cells)]
    reduce_sum x0 -> x1, other arithmetic: none -> 34.4 us  [start_fields_over_axis(): return jnp.sum(lax.all_gather(buf, axis_name=named_axis), axis=0)]
    ppermute x4, waiting for transfers between devices: 2.27 us -> 23.1 us  [shifted_2(): return lax.ppermute(block, axis, route)]
    convert_element_type x50, local copies, waits for them, and re-layouts: 21.1 us -> 2.5 us  [on_device(): grad_volume = conv_valid(padded_cotangent, flipped).astype(jnp.bfloat16)]
    dot_general x24, matrix products: 25.2 us -> 8.38 us  [on_device(): jnp.einsum('hwg,cg->hwc', grad_volume[disp_index].astype(jnp.float32), gr...]
    unnamed x88 -> x64, local copies, waits for them, and re-layouts: 20.9 us -> 11.6 us
  transfers between devices with their start and end apart: 13 -> 13, of which waited for: 5 -> 10; matrix products, arithmetic and copies ran while one was open for 33% -> 8% of each run, Pallas kernels for 0% -> 0%
where the time goes in v1:
time: 826 us; the launch traced here: 812 us
  waiting for transfers between devices  572 us (69%)
  matrix products  76.5 us (9%)
  other arithmetic  54 us (7%)
  local copies, waits for them, and re-layouts  50 us (6%)
  starting transfers between devices  43.9 us (5%)
  between operations  15.8 us (2%)
    all_gather x1, waiting for transfers between devices, start_fields_over_axis(): return jnp.sum(lax.all_gather(buf, axis_name=named_axis), axis=0)  535 us
    transpose x1, matrix products, on_device(): local_grad = jnp.transpose(kernel_raw, (1, 2, 3, 0, 4))  42.7 us
    reduce_sum x1, other arithmetic, start_fields_over_axis(): return jnp.sum(lax.all_gather(buf, axis_name=named_axis), axis=0)  34.4 us
    ppermute x4, waiting for transfers between devices, shifted_2(): return lax.ppermute(block, axis, route)  23.1 us
    ppermute x4, starting transfers between devices, with_halo(): lax.ppermute(tail, axis, [(i, (i + 1) % count) for i in range(ends)])  21.5 us
  transfers between devices with their start and end apart: 13, of which 10 were waited for; matrix products, arithmetic and copies ran while one was open for 8% of the time, Pallas kernels for 0%

profile of v1, /device:TPU:1, one launch (start us, length us, event | category | flops | bytes accessed | tf_op | source)
XLA Modules:
  0.0 812.0 jit_solution(5889189941326507318)
XLA Ops:
  7.2 6.3 collective-permute-start
  13.6 2.9 collective-permute-done
  16.5 5.8 collective-permute-start.1
  22.3 1.5 fusion.45
  23.8 1.1 collective-permute-done.1
  25.0 1.1 constant_dynamic-update-slice_fusion
  26.1 1.4 fusion.44
  28.1 0.5 fusion.42
  29.1 0.5 fusion.40
  30.1 0.5 fusion.38
  32.1 0.5 fusion.34
  33.2 0.5 fusion.32
  35.2 0.5 fusion.28
  36.3 0.5 fusion.26
  37.3 0.5 fusion.24
  38.3 0.5 fusion.22
  39.1 1.3 collective-permute-start.3
  40.4 4.0 collective-permute-start.2
  44.4 1.6 collective-permute-done.3
  46.0 1.5 collective-permute-done.2
  47.5 0.7 copy-done.9
  48.5 1.8 fusion.250
  50.4 2.3 copy.203
  52.7 1.9 collective-permute-start.5
  54.6 0.9 copy.202
  55.5 7.4 collective-permute-start.4
  62.9 7.3 copy.211
  70.2 1.0 copy.205
  71.2 2.0 copy.204
  73.2 3.0 pad_maximum_fusion.1
  76.2 1.5 pad_bitcast_fusion
  77.7 12.4 %copy.210 = bf16[1,26,6,66,40]{4,0,3,2,1:T(2,128)(2,1)} copy(bf16[1,26,6,66,40]{3,4,2,1,0:T(8,128)(2,1)} %pad_bitcast_fusion) | data formatting | bytes 1647360 | tf_op jit(solution)/shard_map/broadcast_in_dim | solution.py:90
  90.1 42.7 %fusion.252 = f32[3,3,3,40,32]{3,4,2,1,0:T(8,128)} fusion(bf16[1,26,6,66,40]{4,0,3,2,1:T(2,128)(2,1)} %copy.210, bf16[1,24,4,64,32]{4,0,3,2,1:T(2,128)(2,1)} %copy.211), kind=kOutput, calls=%fused_computation.321 | convolution fusion | flops 424673280 | bytes 1355136 | tf_op jit(solution)/shard_map/transpose | solution.py:97
  132.8 1.9 copy.212
  134.8 1.3 collective-permute-start.7
  136.1 4.8 collective-permute-start.6
  140.9 3.2 collective-permute-done.7
  144.1 1.5 collective-permute-done.6
  145.6 1.9 collective-permute-start.9
  147.5 5.4 collective-permute-start.8
  152.9 5.8 collective-permute-done.9
  158.7 10.2 %maximum_bitcast_fusion = bf16[24,6,1,66,32]{4,0,3,1,2:T(8,128)(2,1)S(1)} fusion(bf16[24,6,1,32]{3,0,2,1:T(8,128)(2,1)S(1)} %collective-permute-done.9, bf16[24,1,64,32]{3,0,2,1:T(8,128)(2,1)S(1)} %collective-permute-done.7, bf16[24,4,64,32]{3,0,2,1:T(8,128)(2,1)S(1)} %copy.212, bf16[24,1,64,32]{3,0,2,1:T(8,128)(2,1)S(1)} %collective-permute-done.6, ...), kind=kLoop, calls=%fused_computation.66 | loop fusion | flops 1216512 | bytes 1216512 | tf_op jit(solution)/shard_map/broadcast_in_dim | solution.py:46
  170.0 5.4 select_convert_fusion
  175.4 1.2 copy-done.11
  179.8 1.1 fusion.248
  187.5 0.9 convert_multiply_fusion.23
  188.6 2.3 multiply_convert_fusion.1
  191.2 1.0 pad_add_fusion
  192.2 0.8 slice.426
  193.4 1.9 collective-permute-start.10
  195.3 1.3 fusion.257
  196.7 2.8 copy.290
  199.5 2.2 pad.125.clone
  202.2 10.5 %collective-permute-done.10 = f32[4,64,320]{2,1,0:T(8,128)} collective-permute-done((f32[4,64,320]{2,1,0:T(8,128)}, f32[4,64,320]{2,1,0:T(8,128)}, u32[]{:S(2)}, u32[]{:S(2)}) %collective-permute-start.10) | collective-permute-done | bytes 327712 | tf_op jit(solution)/shard_map/ppermute | solution.py:24
  212.7 1.8 slice_add_fusion.1
  214.5 1.9 collective-permute-start.11
  216.4 6.0 select_convert_fusion.1
  222.4 0.7 copy.209
  223.4 1.7 copy.265
  225.1 8.6 %collective-permute-done.11 = f32[4,64,320]{2,1,0:T(8,128)S(1)} collective-permute-done((f32[4,64,320]{2,1,0:T(8,128)}, f32[4,64,320]{2,1,0:T(8,128)S(1)}, u32[]{:S(2)}, u32[]{:S(2)}) %collective-permute-start.11) | collective-permute-done | bytes 327712 | tf_op jit(solution)/shard_map/ppermute | solution.py:24
  233.7 0.7 fusion.70
  234.4 535.1 %all-gather.3.cloned.1.call-done = f32[768,3,3,40,32]{3,4,2,1,0:T(8,128)} async-done(((f32[3,3,3,40,32]{3,4,2,1,0:T(8,128)}), f32[768,3,3,40,32]{3,4,2,1,0:T(8,128)}) %all-gather.3.cloned.1.call-update) | async-done | bytes 35389456 | tf_op jit(solution)/shard_map/all_gather | solution.py:15
  769.6 34.4 %reduce_sum.9 = f32[3,3,3,40,32]{3,4,2,1,0:T(8,128)S(1)} reduce(f32[256,3,3,3,40,32]{4,5,3,2,1,0:T(8,128)} %bitcast.32, f32[]{:T(128)} %constant.31.clone.1), dimensions={0}, to_apply=%region_0.1 | reduce | flops 8812800 | bytes 35527684 | tf_op jit(solution)/shard_map/reduce_sum | solution.py:15
  804.0 0.8 broadcast_multiply_fusion
  (162 shorter events, 19.2 us)
Async XLA Ops:
  7.2 162.7 %copy-start = (bf16[3,3,3,40,32]{3,4,2,1,0:T(8,128)(2,1)S(1)}, bf16[3,3,3,40,32]{3,4,2,1,0:T(8,128)(2,1)}, u32[]{:S(2)}) copy-start(bf16[3,3,3,40,32]{3,4,2,1,0:T(8,128)(2,1)} %param.6) | copy-start | bytes 207364
  7.2 20.4 %copy-start.1 = (bf16[4,64,320]{2,1,0:T(8,128)(2,1)S(1)}, bf16[4,64,320]{2,1,0:T(8,128)(2,1)}, u32[]{:S(2)}) copy-start(bf16[4,64,320]{2,1,0:T(8,128)(2,1)} %param.4) | copy-start | bytes 491524
  7.2 762.4 %all-gather.3.cloned.1.call-start = ((), (), s32[]{:S(2)}) async-start(), calls=%async_computation | async-start | bytes 113688576 | tf_op jit(solution)/shard_map/all_gather | solution.py:15
  7.2 9.3 %collective-permute-start = (bf16[4,64,320]{2,1,0:T(8,128)(2,1)}, bf16[4,64,320]{2,1,0:T(8,128)(2,1)S(1)}, u32[]{:S(2)}, u32[]{:S(2)}) collective-permute-start(bf16[4,64,320]{2,1,0:T(8,128)(2,1)} %param.5), channel_id=1, source_target_pairs={{0,1},{1,2},{2,3},{3,4},{4,5},{5,6},{6,7},{7,8},{8,9},{9,10},{10,1... | collective-permute-start | bytes 491528 | tf_op jit(solution)/shard_map/ppermute | solution.py:24
  16.5 18.2 %copy-start.15 = (bf16[4,64,320]{2,1,0:T(8,128)(2,1)}, bf16[4,64,320]{2,1,0:T(8,128)(2,1)S(1)}, u32[]{:S(2)}) copy-start(bf16[4,64,320]{2,1,0:T(8,128)(2,1)S(1)} %collective-permute-done) | copy-start | bytes 491524
  16.5 8.4 %collective-permute-start.1 = (bf16[4,64,320]{2,1,0:T(8,128)(2,1)S(1)}, bf16[4,64,320]{2,1,0:T(8,128)(2,1)S(1)}, u32[]{:S(2)}, u32[]{:S(2)}) collective-permute-start(bf16[4,64,320]{2,1,0:T(8,128)(2,1)S(1)} %collective-permute-done), channel_id=1, source_target_pairs={{0,1},{1,2},{2,3},{3,4},{4,5},{5,6},{6,7},{7,8},{8,9},{9,10},{10,1... | collective-permute-start | bytes 491528 | tf_op jit(solution)/shard_map/ppermute | solution.py:24
  25.0 13.3 %copy-start.12 = (bf16[4,128,320]{2,1,0:T(8,128)(2,1)}, bf16[4,128,320]{2,1,0:T(8,128)(2,1)S(1)}, u32[]{:S(2)}) copy-start(bf16[4,128,320]{2,1,0:T(8,128)(2,1)S(1)} %get-tuple-element.76) | copy-start | bytes 983044
  39.1 6.9 collective-permute-start.3
  40.4 7.1 collective-permute-start.2
  46.0 1.5 copy-start.7
  47.5 0.7 copy-start.9
  52.7 17.5 %collective-permute-start.5 = (bf16[24,6,1,40]{3,0,2,1:T(8,128)(2,1)S(1)}, bf16[24,6,1,40]{3,0,2,1:T(8,128)(2,1)S(1)}, u32[]{:S(2)}, u32[]{:S(2)}) collective-permute-start(bf16[24,6,1,40]{3,0,2,1:T(8,128)(2,1)S(1)} %copy.203), channel_id=1, source_target_pairs={{1,0},{2,1},{3,2},{4,3},{5,4},{6,5},{7,6},{8,7},{9,8},{10,9},{11,1... | collective-permute-start | bytes 34568 | tf_op jit(solution)/shard_map/ppermute | solution.py:37
  55.5 15.7 %collective-permute-start.4 = (bf16[24,6,1,40]{3,0,2,1:T(8,128)(2,1)S(1)}, bf16[24,6,1,40]{3,0,2,1:T(8,128)(2,1)S(1)}, u32[]{:S(2)}, u32[]{:S(2)}) collective-permute-start(bf16[24,6,1,40]{3,0,2,1:T(8,128)(2,1)S(1)} %copy.202), channel_id=1, source_target_pairs={{0,1},{1,2},{2,3},{3,4},{4,5},{5,6},{6,7},{7,8},{8,9},{9,10},{10,1... | collective-permute-start | bytes 34568 | tf_op jit(solution)/shard_map/ppermute | solution.py:35
  71.2 5.0 copy-start.2
  134.8 9.3 %collective-permute-start.7 = (bf16[24,1,64,32]{3,0,2,1:T(8,128)(2,1)S(1)}, bf16[24,1,64,32]{3,0,2,1:T(8,128)(2,1)S(1)}, u32[]{:S(2)}, u32[]{:S(2)}) collective-permute-start(bf16[24,1,64,32]{3,0,2,1:T(8,128)(2,1)S(1)} %get-tuple-element.47), channel_id=1, source_target_pairs={{32,0},{64,32},{96,64},{128,96},{160,128},{192,160},{224,192},{33,... | collective-permute-start | bytes 294920 | tf_op jit(solution)/shard_map/ppermute | solution.py:37
  136.1 9.4 %collective-permute-start.6 = (bf16[24,1,64,32]{3,0,2,1:T(8,128)(2,1)S(1)}, bf16[24,1,64,32]{3,0,2,1:T(8,128)(2,1)S(1)}, u32[]{:S(2)}, u32[]{:S(2)}) collective-permute-start(bf16[24,1,64,32]{3,0,2,1:T(8,128)(2,1)S(1)} %get-tuple-element.46), channel_id=1, source_target_pairs={{0,32},{32,64},{64,96},{96,128},{128,160},{160,192},{192,224},{1,3... | collective-permute-start | bytes 294920 | tf_op jit(solution)/shard_map/ppermute | solution.py:35
  145.6 13.1 %collective-permute-start.9 = (bf16[24,6,1,32]{3,0,2,1:T(8,128)(2,1)S(1)}, bf16[24,6,1,32]{3,0,2,1:T(8,128)(2,1)S(1)}, u32[]{:S(2)}, u32[]{:S(2)}) collective-permute-start(bf16[24,6,1,32]{3,0,2,1:T(8,128)(2,1)S(1)} %get-tuple-element.21), channel_id=1, source_target_pairs={{1,0},{2,1},{3,2},{4,3},{5,4},{6,5},{7,6},{8,7},{9,8},{10,9},{11,1... | collective-permute-start | bytes 27656 | tf_op jit(solution)/shard_map/ppermute | solution.py:37
  147.5 11.2 %collective-permute-start.8 = (bf16[24,6,1,32]{3,0,2,1:T(8,128)(2,1)S(1)}, bf16[24,6,1,32]{3,0,2,1:T(8,128)(2,1)S(1)}, u32[]{:S(2)}, u32[]{:S(2)}) collective-permute-start(bf16[24,6,1,32]{3,0,2,1:T(8,128)(2,1)S(1)} %get-tuple-element.20), channel_id=1, source_target_pairs={{0,1},{1,2},{2,3},{3,4},{4,5},{5,6},{6,7},{7,8},{8,9},{9,10},{10,1... | collective-permute-start | bytes 27656 | tf_op jit(solution)/shard_map/ppermute | solution.py:35
  169.4 0.7 copy-start.17
  175.4 1.2 copy-start.11
  187.4 1.0 copy-start.13
  187.5 1.1 copy-start.14
  187.5 1.2 copy-start.16
  191.2 4.1 copy-start.3
  191.2 4.1 copy-start.4
  191.2 4.1 copy-start.8
  191.2 4.1 copy-start.10
  192.2 1.2 copy-start.5
  193.4 19.3 %collective-permute-start.10 = (f32[4,64,320]{2,1,0:T(8,128)}, f32[4,64,320]{2,1,0:T(8,128)}, u32[]{:S(2)}, u32[]{:S(2)}) collective-permute-start(f32[4,64,320]{2,1,0:T(8,128)} %slice.426), channel_id=1, source_target_pairs={{1,0},{2,1},{3,2},{4,3},{5,4},{6,5},{7,6},{8,7},{9,8},{10,9},{11,1... | collective-permute-start | bytes 983048 | tf_op jit(solution)/shard_map/ppermute | solution.py:24
  201.7 11.0 %copy-start.6 = (f32[4,192,320]{2,1,0:T(8,128)S(1)}, f32[4,192,320]{2,1,0:T(8,128)}, u32[]{:S(2)}) copy-start(f32[4,192,320]{2,1,0:T(8,128)} %copy-done.5) | copy-start | bytes 2949124
  214.5 19.2 %collective-permute-start.11 = (f32[4,64,320]{2,1,0:T(8,128)}, f32[4,64,320]{2,1,0:T(8,128)S(1)}, u32[]{:S(2)}, u32[]{:S(2)}) collective-permute-start(f32[4,64,320]{2,1,0:T(8,128)} %slice_add_fusion.1), channel_id=1, source_target_pairs={{1,0},{2,1},{3,2},{4,3},{5,4},{6,5},{7,6},{8,7},{9,8},{10,9},{11,1... | collective-permute-start | bytes 983048 | tf_op jit(solution)/shard_map/ppermute | solution.py:24
Sparse Core Ops, SparseCore 0:
  132.9 636.5 all-gather.2
